TPU v7x, 256 devices: a whole 4x4x8 slice. The times are simulated.
256 devices in a mesh: section: 16 (over y, x), expert: 16 (over z, core).
Axes of the slice: x: 4, y: 4, z: 8, core: 2. Of those that a mesh axis runs over, the one named last changes fastest.
Arguments:
- layer_inputs: bfloat16 [16, 16, 128, 4096], P('section', None, 'expert'), may hold values from -6 to 6
- expert_ids: int32 [16, 16, 128, 2], P('section', None, 'expert'), may hold values from 0 to 7, all different within a row; in each aligned block of 8 rows (0 to 7, 8 to 15, ..., all dimensions but the last counted through in order) at most 3 rows name the same one
- gates: bfloat16 [16, 16, 128, 2], P('section', None, 'expert'), may hold values from 0.099609375 to 0.59765625
- w_gate: bfloat16 [16, 4096, 4096], P('section', None, 'expert'), may hold values from -0.09375 to 0.09375
- w_up: bfloat16 [16, 4096, 4096], P('section', None, 'expert'), may hold values from -0.09375 to 0.09375
- w_down: bfloat16 [16, 4096, 4096], P('section', 'expert'), may hold values from -0.25 to 0.25
- out_grad: bfloat16 [16, 128, 4096], P(None, 'expert'), may hold values from -6 to 6
Outputs:
- section_grads: bfloat16 [16, 16, 128, 4096], P('section', None, 'expert')
Inputs may be any that keep to these rules, and one draw needn't show every extreme that they name: `expert_ids`: within one micro-batch of one section, the 8 tokens of one expert index name each expert at most 3 times, and in some such groups one expert exactly 3 times; a token's 2 experts differ.
All inputs are finite; a program needn't handle non-finite values.
Results may differ from a plain program's by a relative error of at most 0.035.
Values may be sent and summed in bfloat16 or wider, within the bound.
A program may use at most 64 MiB of HBM per device.

v0:
```python
import jax
import jax.numpy as jnp
from jax import lax
from jax.sharding import PartitionSpec as P

EXPERTS = 8
CAP = 3


def passed_along(x, axis, by):
    length = lax.axis_size(axis)
    pairs = [(i, i + by) for i in range(length) if 0 <= i + by < length]
    return lax.ppermute(x, axis, pairs)


def selection(choices, capacity):
    token_count, top_count = (choices.shape[-2], choices.shape[-1])
    experts = jnp.arange(EXPERTS, dtype=jnp.int32)
    onehot = (choices[..., None] == experts).astype(jnp.int32)
    leading = onehot.shape[:-3]
    flattened = onehot.reshape(leading + (token_count * top_count, EXPERTS))
    before = jnp.cumsum(flattened, axis=-2) - flattened
    slot_index = jnp.sum((before * flattened).reshape(onehot.shape), axis=-1)
    places = jnp.arange(capacity, dtype=jnp.int32)
    in_slot = (slot_index[..., None] == places).astype(jnp.int32)
    return onehot[..., None] * in_slot[..., None, :]


def on_device(layer_inputs, expert_ids, gates, w_gate, w_up, w_down, out_grad):
    expert_count = lax.axis_size("expert")
    section_count = lax.axis_size("section")
    section_index = lax.axis_index("section")
    inputs = layer_inputs[0]
    gate_slice = w_gate[0]
    up_slice = w_up[0]
    down_slice = w_down[0]
    micro_count, token_count, model_width = inputs.shape
    hidden = gate_slice.shape[1]
    shards = expert_count // EXPERTS
    capacity = CAP
    slot_rows = expert_count * capacity
    contract = (((1,), (1,)), ((), ()))
    selected = selection(expert_ids[0], capacity)
    dispatch = jnp.sum(selected, axis=2).astype(jnp.bfloat16)
    gate_values = gates[0].astype(jnp.float32)
    combine = jnp.sum(selected.astype(jnp.float32) * gate_values[..., None, None], axis=2).astype(
        jnp.bfloat16
    )

    def spread(rows):
        leading = rows.shape[:-3]
        rows = rows.astype(jnp.bfloat16)
        rows = jnp.broadcast_to(
            jnp.expand_dims(rows, -3), leading + (EXPERTS, shards, capacity, model_width)
        )
        return rows.reshape(leading + (expert_count, capacity, model_width))

    def backward_rows(grad_block, act, coef):
        down_grad = lax.dot_general(
            grad_block, down_slice, contract, preferred_element_type=jnp.float32
        )
        dgate = (down_grad * coef).astype(jnp.bfloat16)
        dup = (down_grad * act).astype(jnp.bfloat16)
        total = lax.dot_general(dgate, gate_slice, contract, preferred_element_type=jnp.float32)
        total = total + lax.dot_general(dup, up_slice, contract, preferred_element_type=jnp.float32)
        return total.astype(jnp.bfloat16)

    zeros_back = jnp.zeros((slot_rows, model_width), jnp.bfloat16)
    outgoing = spread(
        jnp.einsum("mtec,mtd->mecd", dispatch, inputs, preferred_element_type=jnp.float32)
    )
    received = lax.all_to_all(outgoing, "expert", split_axis=1, concat_axis=1, tiled=True)
    item_count = received.shape[0]
    row_block = received.reshape(-1, model_width)
    pre_gate = jnp.dot(row_block, gate_slice, preferred_element_type=jnp.float32)
    pre_up = jnp.dot(row_block, up_slice, preferred_element_type=jnp.float32)
    sigmoid_gate = jax.nn.sigmoid(pre_gate)
    act = pre_gate * sigmoid_gate
    coef = pre_up * (sigmoid_gate * (1.0 + pre_gate * (1.0 - sigmoid_gate)))
    act, coef = (act, coef)
    saved = jnp.stack([act, coef]).reshape(2, item_count, slot_rows, hidden)
    act_all = saved[0]
    coef_all = saved[1]

    def tick(tick_index, state_pair):
        incoming, results = state_pair
        micro_index = tick_index - (section_count - 1 - section_index)
        active = (micro_index >= 0) & (micro_index < micro_count)
        micro_slot = jnp.clip(micro_index, 0, micro_count - 1)
        top_grad = lax.dynamic_index_in_dim(out_grad, micro_slot, 0, keepdims=False)
        grad_out = jnp.where(section_index == section_count - 1, top_grad, incoming)
        dispatch_micro = lax.dynamic_index_in_dim(dispatch, micro_slot, 0, keepdims=False)
        combine_micro = lax.dynamic_index_in_dim(combine, micro_slot, 0, keepdims=False)
        grad_rows = spread(
            jnp.einsum("tec,td->ecd", dispatch_micro, grad_out, preferred_element_type=jnp.float32)
        )
        arrived = lax.all_to_all(
            grad_rows, "expert", split_axis=0, concat_axis=0, tiled=True
        ).reshape(slot_rows, model_width)

        def local_saved(row_block):
            act = lax.dynamic_index_in_dim(act_all, micro_slot, 0, keepdims=False)
            coef = lax.dynamic_index_in_dim(coef_all, micro_slot, 0, keepdims=False)
            return backward_rows(row_block, act, coef)

        def skip_saved(row_block):
            return zeros_back

        back = lax.cond(active, local_saved, skip_saved, arrived)
        returned = lax.all_to_all(
            back.reshape(expert_count, capacity, model_width),
            "expert",
            split_axis=0,
            concat_axis=0,
            tiled=True,
        )
        returned = returned.reshape(EXPERTS, shards, capacity, model_width)
        mixed = jnp.einsum(
            "tec,ekcd->td", combine_micro, returned, preferred_element_type=jnp.float32
        )
        grad_in = (grad_out.astype(jnp.float32) + mixed).astype(jnp.bfloat16)
        updated = lax.dynamic_update_index_in_dim(results, grad_in, micro_slot, 0)
        results = jnp.where(active, updated, results)
        passed = passed_along(grad_in, "section", -1)
        return (passed, results)

    initial = (
        jnp.zeros((token_count, model_width), jnp.bfloat16),
        jnp.zeros((micro_count, token_count, model_width), jnp.bfloat16),
    )
    final_state = lax.fori_loop(0, micro_count + section_count - 1, tick, initial)
    return final_state[1][None]


def solution(mesh):
    placed = (
        P("section", None, "expert", None),
        P("section", None, "expert", None),
        P("section", None, "expert", None),
        P("section", None, "expert"),
        P("section", None, "expert"),
        P("section", "expert", None),
        P(None, "expert", None),
    )
    return jax.shard_map(
        on_device,
        mesh=mesh,
        in_specs=placed,
        out_specs=P("section", None, "expert", None),
        check_vma=False,
    )
```

profile of v0, /device:TPU:1, one launch (start us, length us, event | category | flops | bytes accessed | tf_op | source)
XLA Modules:
  0.0 2030.5 jit_solution(850015349437797174)
XLA Ops:
  19.4 137.7 %all-to-all-done.2 = bf16[16,16,3,4096]{3,0,2,1:T(8,128)(2,1)} async-done(((bf16[16,16,3,4096]{3,0,2,1:T(8,128)(2,1)}), bf16[16,16,3,4096]{3,0,2,1:T(8,128)(2,1)}, u32[]{:S(2)}, u32[]{:S(2)}) %all-to-all-start.2) | async-done | bytes 6291488 | tf_op jit(solution)/shard_map/all_to_all | solution.py:72
  191.9 1838.6 %while.17 = (s32[]{:T(128)}, bf16[8,4096]{1,0:T(8,128)(2,1)S(1)}, bf16[16,8,4096]{2,1,0:T(8,128)(2,1)}, pred[]{:T(512)}, s32[]{:T(128)}, /*index=5*/bf16[16,8,40...) while((s32[]{:T(128)}, bf16[8,4096]{1,0:T(8,128)(2,1)S(1)}, ...), condition=%wide.region_8.9_spmd, body=%wide.region_4.8_spmd.sunk | while | flops 306167808 | bytes 32488984 | solution.py:131
  483.4 20.3 %all_to_all.29 = bf16[16,3,4096]{2,1,0:T(4,128)(2,1)S(1)} all-to-all(bf16[16,3,4096]{2,1,0:T(4,128)(2,1)} %reshape.87), channel_id=1, replica_groups=mesh['section'=16,'expert'=16] {'expert'}, dimensions={0} | all-to-all | bytes 786432 | tf_op jit(solution)/shard_map/while/body/eval_jaxpr/all_to_all | solution.py:110
  538.2 20.3 %all_to_all.29 = bf16[16,3,4096]{2,1,0:T(4,128)(2,1)S(1)} all-to-all(bf16[16,3,4096]{2,1,0:T(4,128)(2,1)} %reshape.87), channel_id=1, replica_groups=mesh['section'=16,'expert'=16] {'expert'}, dimensions={0} | all-to-all | bytes 786432 | tf_op jit(solution)/shard_map/while/body/eval_jaxpr/all_to_all | solution.py:110
  593.0 20.3 %all_to_all.29 = bf16[16,3,4096]{2,1,0:T(4,128)(2,1)S(1)} all-to-all(bf16[16,3,4096]{2,1,0:T(4,128)(2,1)} %reshape.87), channel_id=1, replica_groups=mesh['section'=16,'expert'=16] {'expert'}, dimensions={0} | all-to-all | bytes 786432 | tf_op jit(solution)/shard_map/while/body/eval_jaxpr/all_to_all | solution.py:110
  647.7 20.3 %all_to_all.29 = bf16[16,3,4096]{2,1,0:T(4,128)(2,1)S(1)} all-to-all(bf16[16,3,4096]{2,1,0:T(4,128)(2,1)} %reshape.87), channel_id=1, replica_groups=mesh['section'=16,'expert'=16] {'expert'}, dimensions={0} | all-to-all | bytes 786432 | tf_op jit(solution)/shard_map/while/body/eval_jaxpr/all_to_all | solution.py:110
  702.5 20.3 %all_to_all.29 = bf16[16,3,4096]{2,1,0:T(4,128)(2,1)S(1)} all-to-all(bf16[16,3,4096]{2,1,0:T(4,128)(2,1)} %reshape.87), channel_id=1, replica_groups=mesh['section'=16,'expert'=16] {'expert'}, dimensions={0} | all-to-all | bytes 786432 | tf_op jit(solution)/shard_map/while/body/eval_jaxpr/all_to_all | solution.py:110
  757.2 20.3 %all_to_all.29 = bf16[16,3,4096]{2,1,0:T(4,128)(2,1)S(1)} all-to-all(bf16[16,3,4096]{2,1,0:T(4,128)(2,1)} %reshape.87), channel_id=1, replica_groups=mesh['section'=16,'expert'=16] {'expert'}, dimensions={0} | all-to-all | bytes 786432 | tf_op jit(solution)/shard_map/while/body/eval_jaxpr/all_to_all | solution.py:110
  812.0 20.3 %all_to_all.29 = bf16[16,3,4096]{2,1,0:T(4,128)(2,1)S(1)} all-to-all(bf16[16,3,4096]{2,1,0:T(4,128)(2,1)} %reshape.87), channel_id=1, replica_groups=mesh['section'=16,'expert'=16] {'expert'}, dimensions={0} | all-to-all | bytes 786432 | tf_op jit(solution)/shard_map/while/body/eval_jaxpr/all_to_all | solution.py:110
  866.8 20.3 %all_to_all.29 = bf16[16,3,4096]{2,1,0:T(4,128)(2,1)S(1)} all-to-all(bf16[16,3,4096]{2,1,0:T(4,128)(2,1)} %reshape.87), channel_id=1, replica_groups=mesh['section'=16,'expert'=16] {'expert'}, dimensions={0} | all-to-all | bytes 786432 | tf_op jit(solution)/shard_map/while/body/eval_jaxpr/all_to_all | solution.py:110
  921.5 20.3 %all_to_all.29 = bf16[16,3,4096]{2,1,0:T(4,128)(2,1)S(1)} all-to-all(bf16[16,3,4096]{2,1,0:T(4,128)(2,1)} %reshape.87), channel_id=1, replica_groups=mesh['section'=16,'expert'=16] {'expert'}, dimensions={0} | all-to-all | bytes 786432 | tf_op jit(solution)/shard_map/while/body/eval_jaxpr/all_to_all | solution.py:110
  976.3 20.3 %all_to_all.29 = bf16[16,3,4096]{2,1,0:T(4,128)(2,1)S(1)} all-to-all(bf16[16,3,4096]{2,1,0:T(4,128)(2,1)} %reshape.87), channel_id=1, replica_groups=mesh['section'=16,'expert'=16] {'expert'}, dimensions={0} | all-to-all | bytes 786432 | tf_op jit(solution)/shard_map/while/body/eval_jaxpr/all_to_all | solution.py:110
  1000.1 60.6 %collective-permute-done = bf16[8,4096]{1,0:T(8,128)(2,1)S(1)} collective-permute-done((bf16[8,4096]{1,0:T(8,128)(2,1)S(1)}, bf16[8,4096]{1,0:T(8,128)(2,1)S(1)}, u32[]{:S(2)}, u32[]{:S(2)}) %collective-permute-start) | collective-permute-done | bytes 65568 | tf_op jit(solution)/shard_map/while/body/eval_jaxpr/ppermute | solution.py:13
  1091.4 20.3 %all_to_all.29 = bf16[16,3,4096]{2,1,0:T(4,128)(2,1)S(1)} all-to-all(bf16[16,3,4096]{2,1,0:T(4,128)(2,1)} %reshape.87), channel_id=1, replica_groups=mesh['section'=16,'expert'=16] {'expert'}, dimensions={0} | all-to-all | bytes 786432 | tf_op jit(solution)/shard_map/while/body/eval_jaxpr/all_to_all | solution.py:110
  1152.2 20.3 %all_to_all.29 = bf16[16,3,4096]{2,1,0:T(4,128)(2,1)S(1)} all-to-all(bf16[16,3,4096]{2,1,0:T(4,128)(2,1)} %reshape.87), channel_id=1, replica_groups=mesh['section'=16,'expert'=16] {'expert'}, dimensions={0} | all-to-all | bytes 786432 | tf_op jit(solution)/shard_map/while/body/eval_jaxpr/all_to_all | solution.py:110
  1212.9 20.3 %all_to_all.29 = bf16[16,3,4096]{2,1,0:T(4,128)(2,1)S(1)} all-to-all(bf16[16,3,4096]{2,1,0:T(4,128)(2,1)} %reshape.87), channel_id=1, replica_groups=mesh['section'=16,'expert'=16] {'expert'}, dimensions={0} | all-to-all | bytes 786432 | tf_op jit(solution)/shard_map/while/body/eval_jaxpr/all_to_all | solution.py:110
  1273.7 20.3 %all_to_all.29 = bf16[16,3,4096]{2,1,0:T(4,128)(2,1)S(1)} all-to-all(bf16[16,3,4096]{2,1,0:T(4,128)(2,1)} %reshape.87), channel_id=1, replica_groups=mesh['section'=16,'expert'=16] {'expert'}, dimensions={0} | all-to-all | bytes 786432 | tf_op jit(solution)/shard_map/while/body/eval_jaxpr/all_to_all | solution.py:110
  1334.5 20.3 %all_to_all.29 = bf16[16,3,4096]{2,1,0:T(4,128)(2,1)S(1)} all-to-all(bf16[16,3,4096]{2,1,0:T(4,128)(2,1)} %reshape.87), channel_id=1, replica_groups=mesh['section'=16,'expert'=16] {'expert'}, dimensions={0} | all-to-all | bytes 786432 | tf_op jit(solution)/shard_map/while/body/eval_jaxpr/all_to_all | solution.py:110
  1456.0 20.3 %all_to_all.29 = bf16[16,3,4096]{2,1,0:T(4,128)(2,1)S(1)} all-to-all(bf16[16,3,4096]{2,1,0:T(4,128)(2,1)} %reshape.87), channel_id=1, replica_groups=mesh['section'=16,'expert'=16] {'expert'}, dimensions={0} | all-to-all | bytes 786432 | tf_op jit(solution)/shard_map/while/body/eval_jaxpr/all_to_all | solution.py:110
  1516.8 20.3 %all_to_all.29 = bf16[16,3,4096]{2,1,0:T(4,128)(2,1)S(1)} all-to-all(bf16[16,3,4096]{2,1,0:T(4,128)(2,1)} %reshape.87), channel_id=1, replica_groups=mesh['section'=16,'expert'=16] {'expert'}, dimensions={0} | all-to-all | bytes 786432 | tf_op jit(solution)/shard_map/while/body/eval_jaxpr/all_to_all | solution.py:110
  1638.3 20.3 %all_to_all.29 = bf16[16,3,4096]{2,1,0:T(4,128)(2,1)S(1)} all-to-all(bf16[16,3,4096]{2,1,0:T(4,128)(2,1)} %reshape.87), channel_id=1, replica_groups=mesh['section'=16,'expert'=16] {'expert'}, dimensions={0} | all-to-all | bytes 786432 | tf_op jit(solution)/shard_map/while/body/eval_jaxpr/all_to_all | solution.py:110
  1820.6 20.3 %all_to_all.29 = bf16[16,3,4096]{2,1,0:T(4,128)(2,1)S(1)} all-to-all(bf16[16,3,4096]{2,1,0:T(4,128)(2,1)} %reshape.87), channel_id=1, replica_groups=mesh['section'=16,'expert'=16] {'expert'}, dimensions={0} | all-to-all | bytes 786432 | tf_op jit(solution)/shard_map/while/body/eval_jaxpr/all_to_all | solution.py:110
  1942.1 20.3 %all_to_all.29 = bf16[16,3,4096]{2,1,0:T(4,128)(2,1)S(1)} all-to-all(bf16[16,3,4096]{2,1,0:T(4,128)(2,1)} %reshape.87), channel_id=1, replica_groups=mesh['section'=16,'expert'=16] {'expert'}, dimensions={0} | all-to-all | bytes 786432 | tf_op jit(solution)/shard_map/while/body/eval_jaxpr/all_to_all | solution.py:110
  2002.9 20.3 %all_to_all.29 = bf16[16,3,4096]{2,1,0:T(4,128)(2,1)S(1)} all-to-all(bf16[16,3,4096]{2,1,0:T(4,128)(2,1)} %reshape.87), channel_id=1, replica_groups=mesh['section'=16,'expert'=16] {'expert'}, dimensions={0} | all-to-all | bytes 786432 | tf_op jit(solution)/shard_map/while/body/eval_jaxpr/all_to_all | solution.py:110
  (710 shorter events, 1499.2 us)
Async XLA Ops:
  8.5 148.7 %all-to-all-start.2 = ((bf16[16,16,3,4096]{3,0,2,1:T(8,128)(2,1)}), bf16[16,16,3,4096]{3,0,2,1:T(8,128)(2,1)}, u32[]{:S(2)}, u32[]{:S(2)}) async-start(bf16[16,16,3,4096]{3,0,2,1:T(8,128)(2,1)} %bitcast.92), calls=%async_computation.2 | async-start | bytes 12582912 | tf_op jit(solution)/shard_map/all_to_all | solution.py:72
  194.5 22.9 %all-to-all-start = ((bf16[16,3,4096]{2,1,0:T(4,128)(2,1)}), bf16[16,3,4096]{2,1,0:T(4,128)(2,1)}, u32[]{:S(2)}, u32[]{:S(2)}) async-start(bf16[16,3,4096]{2,1,0:T(4,128)(2,1)} %bitcast.91), calls=%async_computation | async-start | bytes 1048576 | tf_op jit(solution)/shard_map/while/body/eval_jaxpr/all_to_all | solution.py:97
  248.4 21.6 %all-to-all-start = ((bf16[16,3,4096]{2,1,0:T(4,128)(2,1)}), bf16[16,3,4096]{2,1,0:T(4,128)(2,1)}, u32[]{:S(2)}, u32[]{:S(2)}) async-start(bf16[16,3,4096]{2,1,0:T(4,128)(2,1)} %bitcast.91), calls=%async_computation | async-start | bytes 1048576 | tf_op jit(solution)/shard_map/while/body/eval_jaxpr/all_to_all | solution.py:97
  301.0 21.7 %all-to-all-start = ((bf16[16,3,4096]{2,1,0:T(4,128)(2,1)}), bf16[16,3,4096]{2,1,0:T(4,128)(2,1)}, u32[]{:S(2)}, u32[]{:S(2)}) async-start(bf16[16,3,4096]{2,1,0:T(4,128)(2,1)} %bitcast.91), calls=%async_computation | async-start | bytes 1048576 | tf_op jit(solution)/shard_map/while/body/eval_jaxpr/all_to_all | solution.py:97
  353.6 21.7 %all-to-all-start = ((bf16[16,3,4096]{2,1,0:T(4,128)(2,1)}), bf16[16,3,4096]{2,1,0:T(4,128)(2,1)}, u32[]{:S(2)}, u32[]{:S(2)}) async-start(bf16[16,3,4096]{2,1,0:T(4,128)(2,1)} %bitcast.91), calls=%async_computation | async-start | bytes 1048576 | tf_op jit(solution)/shard_map/while/body/eval_jaxpr/all_to_all | solution.py:97
  406.3 21.5 %all-to-all-start = ((bf16[16,3,4096]{2,1,0:T(4,128)(2,1)}), bf16[16,3,4096]{2,1,0:T(4,128)(2,1)}, u32[]{:S(2)}, u32[]{:S(2)}) async-start(bf16[16,3,4096]{2,1,0:T(4,128)(2,1)} %bitcast.91), calls=%async_computation | async-start | bytes 1048576 | tf_op jit(solution)/shard_map/while/body/eval_jaxpr/all_to_all | solution.py:97
  515.8 21.3 %all-to-all-start = ((bf16[16,3,4096]{2,1,0:T(4,128)(2,1)}), bf16[16,3,4096]{2,1,0:T(4,128)(2,1)}, u32[]{:S(2)}, u32[]{:S(2)}) async-start(bf16[16,3,4096]{2,1,0:T(4,128)(2,1)} %bitcast.91), calls=%async_computation | async-start | bytes 1048576 | tf_op jit(solution)/shard_map/while/body/eval_jaxpr/all_to_all | solution.py:97
  998.8 61.9 %collective-permute-start = (bf16[8,4096]{1,0:T(8,128)(2,1)S(1)}, bf16[8,4096]{1,0:T(8,128)(2,1)S(1)}, u32[]{:S(2)}, u32[]{:S(2)}) collective-permute-start(bf16[8,4096]{1,0:T(8,128)(2,1)S(1)} %get-tuple-element.441), channel_id=1, source_target_pairs={{16,0},{32,16},{48,32},{64,48},{80,64},{96,80},{112,96},{128,112},... | collective-permute-start | bytes 196616 | tf_op jit(solution)/shard_map/while/body/eval_jaxpr/ppermute | solution.py:13
  1062.9 21.4 %all-to-all-start = ((bf16[16,3,4096]{2,1,0:T(4,128)(2,1)}), bf16[16,3,4096]{2,1,0:T(4,128)(2,1)}, u32[]{:S(2)}, u32[]{:S(2)}) async-start(bf16[16,3,4096]{2,1,0:T(4,128)(2,1)} %bitcast.91), calls=%async_computation | async-start | bytes 1048576 | tf_op jit(solution)/shard_map/while/body/eval_jaxpr/all_to_all | solution.py:97
  1123.7 21.4 %all-to-all-start = ((bf16[16,3,4096]{2,1,0:T(4,128)(2,1)}), bf16[16,3,4096]{2,1,0:T(4,128)(2,1)}, u32[]{:S(2)}, u32[]{:S(2)}) async-start(bf16[16,3,4096]{2,1,0:T(4,128)(2,1)} %bitcast.91), calls=%async_computation | async-start | bytes 1048576 | tf_op jit(solution)/shard_map/while/body/eval_jaxpr/all_to_all | solution.py:97
  1184.4 21.4 %all-to-all-start = ((bf16[16,3,4096]{2,1,0:T(4,128)(2,1)}), bf16[16,3,4096]{2,1,0:T(4,128)(2,1)}, u32[]{:S(2)}, u32[]{:S(2)}) async-start(bf16[16,3,4096]{2,1,0:T(4,128)(2,1)} %bitcast.91), calls=%async_computation | async-start | bytes 1048576 | tf_op jit(solution)/shard_map/while/body/eval_jaxpr/all_to_all | solution.py:97
  1245.2 21.4 %all-to-all-start = ((bf16[16,3,4096]{2,1,0:T(4,128)(2,1)}), bf16[16,3,4096]{2,1,0:T(4,128)(2,1)}, u32[]{:S(2)}, u32[]{:S(2)}) async-start(bf16[16,3,4096]{2,1,0:T(4,128)(2,1)} %bitcast.91), calls=%async_computation | async-start | bytes 1048576 | tf_op jit(solution)/shard_map/while/body/eval_jaxpr/all_to_all | solution.py:97
  1306.0 21.4 %all-to-all-start = ((bf16[16,3,4096]{2,1,0:T(4,128)(2,1)}), bf16[16,3,4096]{2,1,0:T(4,128)(2,1)}, u32[]{:S(2)}, u32[]{:S(2)}) async-start(bf16[16,3,4096]{2,1,0:T(4,128)(2,1)} %bitcast.91), calls=%async_computation | async-start | bytes 1048576 | tf_op jit(solution)/shard_map/while/body/eval_jaxpr/all_to_all | solution.py:97
  1366.7 21.4 %all-to-all-start = ((bf16[16,3,4096]{2,1,0:T(4,128)(2,1)}), bf16[16,3,4096]{2,1,0:T(4,128)(2,1)}, u32[]{:S(2)}, u32[]{:S(2)}) async-start(bf16[16,3,4096]{2,1,0:T(4,128)(2,1)} %bitcast.91), calls=%async_computation | async-start | bytes 1048576 | tf_op jit(solution)/shard_map/while/body/eval_jaxpr/all_to_all | solution.py:97
  1427.6 21.4 %all-to-all-start = ((bf16[16,3,4096]{2,1,0:T(4,128)(2,1)}), bf16[16,3,4096]{2,1,0:T(4,128)(2,1)}, u32[]{:S(2)}, u32[]{:S(2)}) async-start(bf16[16,3,4096]{2,1,0:T(4,128)(2,1)} %bitcast.91), calls=%async_computation | async-start | bytes 1048576 | tf_op jit(solution)/shard_map/while/body/eval_jaxpr/all_to_all | solution.py:97
  1488.3 21.4 %all-to-all-start = ((bf16[16,3,4096]{2,1,0:T(4,128)(2,1)}), bf16[16,3,4096]{2,1,0:T(4,128)(2,1)}, u32[]{:S(2)}, u32[]{:S(2)}) async-start(bf16[16,3,4096]{2,1,0:T(4,128)(2,1)} %bitcast.91), calls=%async_computation | async-start | bytes 1048576 | tf_op jit(solution)/shard_map/while/body/eval_jaxpr/all_to_all | solution.py:97
  1549.0 21.4 %all-to-all-start = ((bf16[16,3,4096]{2,1,0:T(4,128)(2,1)}), bf16[16,3,4096]{2,1,0:T(4,128)(2,1)}, u32[]{:S(2)}, u32[]{:S(2)}) async-start(bf16[16,3,4096]{2,1,0:T(4,128)(2,1)} %bitcast.91), calls=%async_computation | async-start | bytes 1048576 | tf_op jit(solution)/shard_map/while/body/eval_jaxpr/all_to_all | solution.py:97
  1609.8 21.4 %all-to-all-start = ((bf16[16,3,4096]{2,1,0:T(4,128)(2,1)}), bf16[16,3,4096]{2,1,0:T(4,128)(2,1)}, u32[]{:S(2)}, u32[]{:S(2)}) async-start(bf16[16,3,4096]{2,1,0:T(4,128)(2,1)} %bitcast.91), calls=%async_computation | async-start | bytes 1048576 | tf_op jit(solution)/shard_map/while/body/eval_jaxpr/all_to_all | solution.py:97
  1670.6 21.4 %all-to-all-start = ((bf16[16,3,4096]{2,1,0:T(4,128)(2,1)}), bf16[16,3,4096]{2,1,0:T(4,128)(2,1)}, u32[]{:S(2)}, u32[]{:S(2)}) async-start(bf16[16,3,4096]{2,1,0:T(4,128)(2,1)} %bitcast.91), calls=%async_computation | async-start | bytes 1048576 | tf_op jit(solution)/shard_map/while/body/eval_jaxpr/all_to_all | solution.py:97
  1731.3 21.4 %all-to-all-start = ((bf16[16,3,4096]{2,1,0:T(4,128)(2,1)}), bf16[16,3,4096]{2,1,0:T(4,128)(2,1)}, u32[]{:S(2)}, u32[]{:S(2)}) async-start(bf16[16,3,4096]{2,1,0:T(4,128)(2,1)} %bitcast.91), calls=%async_computation | async-start | bytes 1048576 | tf_op jit(solution)/shard_map/while/body/eval_jaxpr/all_to_all | solution.py:97
  1792.1 21.4 %all-to-all-start = ((bf16[16,3,4096]{2,1,0:T(4,128)(2,1)}), bf16[16,3,4096]{2,1,0:T(4,128)(2,1)}, u32[]{:S(2)}, u32[]{:S(2)}) async-start(bf16[16,3,4096]{2,1,0:T(4,128)(2,1)} %bitcast.91), calls=%async_computation | async-start | bytes 1048576 | tf_op jit(solution)/shard_map/while/body/eval_jaxpr/all_to_all | solution.py:97
  1852.9 21.4 %all-to-all-start = ((bf16[16,3,4096]{2,1,0:T(4,128)(2,1)}), bf16[16,3,4096]{2,1,0:T(4,128)(2,1)}, u32[]{:S(2)}, u32[]{:S(2)}) async-start(bf16[16,3,4096]{2,1,0:T(4,128)(2,1)} %bitcast.91), calls=%async_computation | async-start | bytes 1048576 | tf_op jit(solution)/shard_map/while/body/eval_jaxpr/all_to_all | solution.py:97
  1913.7 21.4 %all-to-all-start = ((bf16[16,3,4096]{2,1,0:T(4,128)(2,1)}), bf16[16,3,4096]{2,1,0:T(4,128)(2,1)}, u32[]{:S(2)}, u32[]{:S(2)}) async-start(bf16[16,3,4096]{2,1,0:T(4,128)(2,1)} %bitcast.91), calls=%async_computation | async-start | bytes 1048576 | tf_op jit(solution)/shard_map/while/body/eval_jaxpr/all_to_all | solution.py:97
  1974.4 21.4 %all-to-all-start = ((bf16[16,3,4096]{2,1,0:T(4,128)(2,1)}), bf16[16,3,4096]{2,1,0:T(4,128)(2,1)}, u32[]{:S(2)}, u32[]{:S(2)}) async-start(bf16[16,3,4096]{2,1,0:T(4,128)(2,1)} %bitcast.91), calls=%async_computation | async-start | bytes 1048576 | tf_op jit(solution)/shard_map/while/body/eval_jaxpr/all_to_all | solution.py:97
  (170 other events, 2955.4 us)
where the time goes:
time: 2040 us; the launch traced here: 2030 us
  waiting for transfers between devices  909 us (45%)
  blocking collectives  630 us (31%)
  starting transfers between devices  180 us (9%)
  matrix products  160 us (8%)
  local copies, waits for them, and re-layouts  137 us (7%)
    all_to_all x31, blocking collectives, tick(): lax.all_to_all(back.reshape(expert_count, capacity, model_width), 'expert...  630 us
    all_to_all x31, waiting for transfers between devices, tick(): lax.all_to_all(grad_rows, 'expert', split_axis=0, concat_axis=0, tiled=True)  534 us
    ppermute x31, waiting for transfers between devices, passed_along(): return lax.ppermute(x, axis, pairs)  237 us
    all_to_all x1, waiting for transfers between devices, on_device(): lax.all_to_all(outgoing, 'expert', split_axis=1, concat_axis=1, tiled=True)  138 us
    all_to_all x31, starting transfers between devices, tick(): lax.all_to_all(grad_rows, 'expert', split_axis=0, concat_axis=0, tiled=True)  130 us
    dot_general x31, matrix products, tick(): jnp.einsum('tec,ekcd->td', combine_micro, returned, preferred_element_typ...  56.5 us
  transfers between devices with their start and end apart: 63, of which 63 were waited for; matrix products, arithmetic and copies ran while one was open for 0% of the time, Pallas kernels for 0%

commit v1 on v0

--- a/solution.py
+++ b/solution.py
@@ -69,7 +69,10 @@
     outgoing = spread(
         jnp.einsum("mtec,mtd->mecd", dispatch, inputs, preferred_element_type=jnp.float32)
     )
-    received = lax.all_to_all(outgoing, "expert", split_axis=1, concat_axis=1, tiled=True)
+    size = lax.axis_size("expert")
+    shards_2 = jnp.stack(jnp.split(outgoing, size, axis=1), axis=0)
+    shards_2 = lax.all_to_all(shards_2, "expert", split_axis=0, concat_axis=0)
+    received = jnp.concatenate(shards_2, axis=1)
     item_count = received.shape[0]
     row_block = received.reshape(-1, model_width)
     pre_gate = jnp.dot(row_block, gate_slice, preferred_element_type=jnp.float32)

time: 2040 us -> 2050 us (level)
  no operation moved by 1% of the time
where the time goes in v1:
time: 2050 us; the launch traced here: 2040 us
  waiting for transfers between devices  909 us (44%)
  blocking collectives  625 us (30%)
  starting transfers between devices  179 us (9%)
  matrix products  174 us (8%)
  local copies, waits for them, and re-layouts  134 us (7%)
    all_to_all x31, blocking collectives, tick(): lax.all_to_all(back.reshape(expert_count, capacity, model_width), 'expert...  625 us
    all_to_all x31, waiting for transfers between devices, tick(): lax.all_to_all(grad_rows, 'expert', split_axis=0, concat_axis=0, tiled=True)  534 us
    ppermute x31, waiting for transfers between devices, passed_along(): return lax.ppermute(x, axis, pairs)  237 us
    all_to_all x1, waiting for transfers between devices, on_device(): shards_2 = lax.all_to_all(shards_2, 'expert', split_axis=0, concat_axis=0)  138 us
    all_to_all x31, starting transfers between devices, tick(): lax.all_to_all(grad_rows, 'expert', split_axis=0, concat_axis=0, tiled=True)  130 us
    dot_general x31, matrix products, tick(): jnp.einsum('tec,ekcd->td', combine_micro, returned, preferred_element_typ...  56.5 us
  transfers between devices with their start and end apart: 63, of which 63 were waited for; matrix products, arithmetic and copies ran while one was open for 0% of the time, Pallas kernels for 0%

profile of v1, /device:TPU:1, one launch (start us, length us, event | category | flops | bytes accessed | tf_op | source)
XLA Modules:
  0.0 2036.5 jit_solution(7968287910833695247)
XLA Ops:
  30.8 137.7 %all-to-all-done.2 = bf16[16,16,1,3,4096]{4,1,3,2,0:T(8,128)(2,1)} async-done(((bf16[16,16,1,3,4096]{4,1,3,2,0:T(8,128)(2,1)}), bf16[16,16,1,3,4096]{4,1,3,2,0:T(8,128)(2,1)}, u32[]{:S(2)}, u32[]{:S(2)}) %all-to-all-start.2) | async-done | bytes 6291488 | tf_op jit(solution)/shard_map/all_to_all | solution.py:74
  203.3 1833.2 %while.17 = (s32[]{:T(128)}, bf16[8,4096]{1,0:T(8,128)(2,1)S(1)}, bf16[16,8,4096]{2,1,0:T(8,128)(2,1)}, pred[]{:T(512)}, s32[]{:T(128)}, /*index=5*/bf16[16,8,40...) while((s32[]{:T(128)}, bf16[8,4096]{1,0:T(8,128)(2,1)S(1)}, ...), condition=%wide.region_8.9_spmd, body=%wide.region_4.8_spmd.sunk | while | flops 306167808 | bytes 24051140 | solution.py:134
  282.2 20.2 all_to_all.29
  334.7 20.2 all_to_all.29
  387.2 20.2 all_to_all.29
  439.5 20.2 all_to_all.29
  493.9 20.2 all_to_all.29
  548.5 20.2 all_to_all.29
  603.1 20.2 all_to_all.29
  657.6 20.2 all_to_all.29
  712.2 20.2 all_to_all.29
  766.8 20.2 all_to_all.29
  821.4 20.2 all_to_all.29
  876.0 20.2 all_to_all.29
  930.6 20.2 all_to_all.29
  985.1 20.2 all_to_all.29
  1008.8 60.7 %collective-permute-done = bf16[8,4096]{1,0:T(8,128)(2,1)S(1)} collective-permute-done((bf16[8,4096]{1,0:T(8,128)(2,1)S(1)}, bf16[8,4096]{1,0:T(8,128)(2,1)S(1)}, u32[]{:S(2)}, u32[]{:S(2)}) %collective-permute-start) | collective-permute-done | bytes 65568 | tf_op jit(solution)/shard_map/while/body/eval_jaxpr/ppermute | solution.py:13
  1100.2 20.2 all_to_all.29
  1160.7 20.2 all_to_all.29
  1221.3 20.2 all_to_all.29
  1281.9 20.2 all_to_all.29
  1645.5 20.2 all_to_all.29
  1827.2 20.2 all_to_all.29
  2009.0 20.2 all_to_all.29
  (570 shorter events, 1508.7 us)
Async XLA Ops:
  19.8 148.7 %all-to-all-start.2 = ((bf16[16,16,1,3,4096]{4,1,3,2,0:T(8,128)(2,1)}), bf16[16,16,1,3,4096]{4,1,3,2,0:T(8,128)(2,1)}, u32[]{:S(2)}, u32[]{:S(2)}) async-start(bf16[16,16,1,3,4096]{4,1,3,2,0:T(8,128)(2,1)} %fusion.22), calls=%async_computation.2 | async-start | bytes 12582912 | tf_op jit(solution)/shard_map/all_to_all | solution.py:74
  205.8 22.9 %all-to-all-start = ((bf16[16,3,4096]{2,1,0:T(4,128)(2,1)}), bf16[16,3,4096]{2,1,0:T(4,128)(2,1)}, u32[]{:S(2)}, u32[]{:S(2)}) async-start(bf16[16,3,4096]{2,1,0:T(4,128)(2,1)} %bitcast.158), calls=%async_computation | async-start | bytes 1048576 | tf_op jit(solution)/shard_map/while/body/eval_jaxpr/all_to_all | solution.py:100
  259.5 21.6 %all-to-all-start = ((bf16[16,3,4096]{2,1,0:T(4,128)(2,1)}), bf16[16,3,4096]{2,1,0:T(4,128)(2,1)}, u32[]{:S(2)}, u32[]{:S(2)}) async-start(bf16[16,3,4096]{2,1,0:T(4,128)(2,1)} %bitcast.158), calls=%async_computation | async-start | bytes 1048576 | tf_op jit(solution)/shard_map/while/body/eval_jaxpr/all_to_all | solution.py:100
  312.0 21.6 %all-to-all-start = ((bf16[16,3,4096]{2,1,0:T(4,128)(2,1)}), bf16[16,3,4096]{2,1,0:T(4,128)(2,1)}, u32[]{:S(2)}, u32[]{:S(2)}) async-start(bf16[16,3,4096]{2,1,0:T(4,128)(2,1)} %bitcast.158), calls=%async_computation | async-start | bytes 1048576 | tf_op jit(solution)/shard_map/while/body/eval_jaxpr/all_to_all | solution.py:100
  364.4 21.6 %all-to-all-start = ((bf16[16,3,4096]{2,1,0:T(4,128)(2,1)}), bf16[16,3,4096]{2,1,0:T(4,128)(2,1)}, u32[]{:S(2)}, u32[]{:S(2)}) async-start(bf16[16,3,4096]{2,1,0:T(4,128)(2,1)} %bitcast.158), calls=%async_computation | async-start | bytes 1048576 | tf_op jit(solution)/shard_map/while/body/eval_jaxpr/all_to_all | solution.py:100
  416.9 21.5 %all-to-all-start = ((bf16[16,3,4096]{2,1,0:T(4,128)(2,1)}), bf16[16,3,4096]{2,1,0:T(4,128)(2,1)}, u32[]{:S(2)}, u32[]{:S(2)}) async-start(bf16[16,3,4096]{2,1,0:T(4,128)(2,1)} %bitcast.158), calls=%async_computation | async-start | bytes 1048576 | tf_op jit(solution)/shard_map/while/body/eval_jaxpr/all_to_all | solution.py:100
  471.5 21.4 %all-to-all-start = ((bf16[16,3,4096]{2,1,0:T(4,128)(2,1)}), bf16[16,3,4096]{2,1,0:T(4,128)(2,1)}, u32[]{:S(2)}, u32[]{:S(2)}) async-start(bf16[16,3,4096]{2,1,0:T(4,128)(2,1)} %bitcast.158), calls=%async_computation | async-start | bytes 1048576 | tf_op jit(solution)/shard_map/while/body/eval_jaxpr/all_to_all | solution.py:100
  526.1 21.4 %all-to-all-start = ((bf16[16,3,4096]{2,1,0:T(4,128)(2,1)}), bf16[16,3,4096]{2,1,0:T(4,128)(2,1)}, u32[]{:S(2)}, u32[]{:S(2)}) async-start(bf16[16,3,4096]{2,1,0:T(4,128)(2,1)} %bitcast.158), calls=%async_computation | async-start | bytes 1048576 | tf_op jit(solution)/shard_map/while/body/eval_jaxpr/all_to_all | solution.py:100
  580.6 21.4 %all-to-all-start = ((bf16[16,3,4096]{2,1,0:T(4,128)(2,1)}), bf16[16,3,4096]{2,1,0:T(4,128)(2,1)}, u32[]{:S(2)}, u32[]{:S(2)}) async-start(bf16[16,3,4096]{2,1,0:T(4,128)(2,1)} %bitcast.158), calls=%async_computation | async-start | bytes 1048576 | tf_op jit(solution)/shard_map/while/body/eval_jaxpr/all_to_all | solution.py:100
  799.0 21.4 %all-to-all-start = ((bf16[16,3,4096]{2,1,0:T(4,128)(2,1)}), bf16[16,3,4096]{2,1,0:T(4,128)(2,1)}, u32[]{:S(2)}, u32[]{:S(2)}) async-start(bf16[16,3,4096]{2,1,0:T(4,128)(2,1)} %bitcast.158), calls=%async_computation | async-start | bytes 1048576 | tf_op jit(solution)/shard_map/while/body/eval_jaxpr/all_to_all | solution.py:100
  853.6 21.4 %all-to-all-start = ((bf16[16,3,4096]{2,1,0:T(4,128)(2,1)}), bf16[16,3,4096]{2,1,0:T(4,128)(2,1)}, u32[]{:S(2)}, u32[]{:S(2)}) async-start(bf16[16,3,4096]{2,1,0:T(4,128)(2,1)} %bitcast.158), calls=%async_computation | async-start | bytes 1048576 | tf_op jit(solution)/shard_map/while/body/eval_jaxpr/all_to_all | solution.py:100
  1007.5 62.0 %collective-permute-start = (bf16[8,4096]{1,0:T(8,128)(2,1)S(1)}, bf16[8,4096]{1,0:T(8,128)(2,1)S(1)}, u32[]{:S(2)}, u32[]{:S(2)}) collective-permute-start(bf16[8,4096]{1,0:T(8,128)(2,1)S(1)} %get-tuple-element.441), channel_id=1, source_target_pairs={{16,0},{32,16},{48,32},{64,48},{80,64},{96,80},{112,96},{128,112},... | collective-permute-start | bytes 196616 | tf_op jit(solution)/shard_map/while/body/eval_jaxpr/ppermute | solution.py:13
  1071.7 21.4 %all-to-all-start = ((bf16[16,3,4096]{2,1,0:T(4,128)(2,1)}), bf16[16,3,4096]{2,1,0:T(4,128)(2,1)}, u32[]{:S(2)}, u32[]{:S(2)}) async-start(bf16[16,3,4096]{2,1,0:T(4,128)(2,1)} %bitcast.158), calls=%async_computation | async-start | bytes 1048576 | tf_op jit(solution)/shard_map/while/body/eval_jaxpr/all_to_all | solution.py:100
  1132.3 21.4 %all-to-all-start = ((bf16[16,3,4096]{2,1,0:T(4,128)(2,1)}), bf16[16,3,4096]{2,1,0:T(4,128)(2,1)}, u32[]{:S(2)}, u32[]{:S(2)}) async-start(bf16[16,3,4096]{2,1,0:T(4,128)(2,1)} %bitcast.158), calls=%async_computation | async-start | bytes 1048576 | tf_op jit(solution)/shard_map/while/body/eval_jaxpr/all_to_all | solution.py:100
  1253.5 21.4 %all-to-all-start = ((bf16[16,3,4096]{2,1,0:T(4,128)(2,1)}), bf16[16,3,4096]{2,1,0:T(4,128)(2,1)}, u32[]{:S(2)}, u32[]{:S(2)}) async-start(bf16[16,3,4096]{2,1,0:T(4,128)(2,1)} %bitcast.158), calls=%async_computation | async-start | bytes 1048576 | tf_op jit(solution)/shard_map/while/body/eval_jaxpr/all_to_all | solution.py:100
  1314.1 21.4 %all-to-all-start = ((bf16[16,3,4096]{2,1,0:T(4,128)(2,1)}), bf16[16,3,4096]{2,1,0:T(4,128)(2,1)}, u32[]{:S(2)}, u32[]{:S(2)}) async-start(bf16[16,3,4096]{2,1,0:T(4,128)(2,1)} %bitcast.158), calls=%async_computation | async-start | bytes 1048576 | tf_op jit(solution)/shard_map/while/body/eval_jaxpr/all_to_all | solution.py:100
  1435.3 21.4 %all-to-all-start = ((bf16[16,3,4096]{2,1,0:T(4,128)(2,1)}), bf16[16,3,4096]{2,1,0:T(4,128)(2,1)}, u32[]{:S(2)}, u32[]{:S(2)}) async-start(bf16[16,3,4096]{2,1,0:T(4,128)(2,1)} %bitcast.158), calls=%async_computation | async-start | bytes 1048576 | tf_op jit(solution)/shard_map/while/body/eval_jaxpr/all_to_all | solution.py:100
  1495.8 21.4 %all-to-all-start = ((bf16[16,3,4096]{2,1,0:T(4,128)(2,1)}), bf16[16,3,4096]{2,1,0:T(4,128)(2,1)}, u32[]{:S(2)}, u32[]{:S(2)}) async-start(bf16[16,3,4096]{2,1,0:T(4,128)(2,1)} %bitcast.158), calls=%async_computation | async-start | bytes 1048576 | tf_op jit(solution)/shard_map/while/body/eval_jaxpr/all_to_all | solution.py:100
  1617.0 21.4 %all-to-all-start = ((bf16[16,3,4096]{2,1,0:T(4,128)(2,1)}), bf16[16,3,4096]{2,1,0:T(4,128)(2,1)}, u32[]{:S(2)}, u32[]{:S(2)}) async-start(bf16[16,3,4096]{2,1,0:T(4,128)(2,1)} %bitcast.158), calls=%async_computation | async-start | bytes 1048576 | tf_op jit(solution)/shard_map/while/body/eval_jaxpr/all_to_all | solution.py:100
  1677.6 21.4 %all-to-all-start = ((bf16[16,3,4096]{2,1,0:T(4,128)(2,1)}), bf16[16,3,4096]{2,1,0:T(4,128)(2,1)}, u32[]{:S(2)}, u32[]{:S(2)}) async-start(bf16[16,3,4096]{2,1,0:T(4,128)(2,1)} %bitcast.158), calls=%async_computation | async-start | bytes 1048576 | tf_op jit(solution)/shard_map/while/body/eval_jaxpr/all_to_all | solution.py:100
  1798.8 21.4 %all-to-all-start = ((bf16[16,3,4096]{2,1,0:T(4,128)(2,1)}), bf16[16,3,4096]{2,1,0:T(4,128)(2,1)}, u32[]{:S(2)}, u32[]{:S(2)}) async-start(bf16[16,3,4096]{2,1,0:T(4,128)(2,1)} %bitcast.158), calls=%async_computation | async-start | bytes 1048576 | tf_op jit(solution)/shard_map/while/body/eval_jaxpr/all_to_all | solution.py:100
  1859.4 21.4 %all-to-all-start = ((bf16[16,3,4096]{2,1,0:T(4,128)(2,1)}), bf16[16,3,4096]{2,1,0:T(4,128)(2,1)}, u32[]{:S(2)}, u32[]{:S(2)}) async-start(bf16[16,3,4096]{2,1,0:T(4,128)(2,1)} %bitcast.158), calls=%async_computation | async-start | bytes 1048576 | tf_op jit(solution)/shard_map/while/body/eval_jaxpr/all_to_all | solution.py:100
  1920.0 21.4 %all-to-all-start = ((bf16[16,3,4096]{2,1,0:T(4,128)(2,1)}), bf16[16,3,4096]{2,1,0:T(4,128)(2,1)}, u32[]{:S(2)}, u32[]{:S(2)}) async-start(bf16[16,3,4096]{2,1,0:T(4,128)(2,1)} %bitcast.158), calls=%async_computation | async-start | bytes 1048576 | tf_op jit(solution)/shard_map/while/body/eval_jaxpr/all_to_all | solution.py:100
  1980.6 21.4 %all-to-all-start = ((bf16[16,3,4096]{2,1,0:T(4,128)(2,1)}), bf16[16,3,4096]{2,1,0:T(4,128)(2,1)}, u32[]{:S(2)}, u32[]{:S(2)}) async-start(bf16[16,3,4096]{2,1,0:T(4,128)(2,1)} %bitcast.158), calls=%async_computation | async-start | bytes 1048576 | tf_op jit(solution)/shard_map/while/body/eval_jaxpr/all_to_all | solution.py:100
  (92 other events, 1234.2 us)
